TPU v7x, 32 devices: a whole 2x2x4 slice. The times are simulated.
32 devices in a mesh: group: 2 (over y), seq: 16 (over z, x, core).
Axes of the slice: x: 2, y: 2, z: 4, core: 2. Of those that a mesh axis runs over, the one named last changes fastest.
Arguments:
- ssm_inputs: bfloat16 [4096, 8192], P(('group', 'seq')), parts along dimension 0, may hold values from -6 to 6
- gate_inputs: bfloat16 [4096, 8192], P(('group', 'seq')), parts along dimension 0, may hold values from -81 to 81
- write_keys: bfloat16 [4096, 1024], P(('group', 'seq')), parts along dimension 0, may hold values from -6 to 6
- read_queries: bfloat16 [4096, 1024], P(('group', 'seq')), parts along dimension 0, may hold values from -6 to 6
- step_size: float32 [4096, 128], P(('group', 'seq')), parts along dimension 0, may hold values from 0.003 to 0.3
- decay_rate: float32 [128], replicated, may hold values from 1e-06 to 1.6
- skip_gain: float32 [128], replicated, may hold values from 0.5 to 2
- norm_gain: float32 [8192], replicated, may hold values from 0.5 to 1.5
- query_proj: bfloat16 [4096, 4096], P(('group', 'seq')), parts along dimension 0, may hold values from -9 to 9
- key_proj: bfloat16 [4096, 512], P(('group', 'seq')), parts along dimension 0, may hold values from -9 to 9
- value_proj: bfloat16 [4096, 512], P(('group', 'seq')), parts along dimension 0, may hold values from -6 to 6
- row_ids: int32 [4096], P(('group', 'seq')), parts along dimension 0, may hold values from 0 to 31, as said below
- partners: int32 [32, 4], P(('group', 'seq')), parts along dimension 0, may hold values from -1 to 14, as said below
Outputs:
- mixer_out: bfloat16 [4096, 8192], P(('group', 'seq')), parts along dimension 0
- attention_out: bfloat16 [4096, 4096], P(('group', 'seq')), parts along dimension 0
There are 2 independent parts, one for each index of `group`. A program takes and returns all parts, laid end to end along the dimension named above; an argument that names none is the same for every part. Nothing has to cross between parts.
Inputs may be any that keep to these rules, and one draw needn't show every extreme that they name: row_ids starts at 0 and rises by 0 or 1 from one token to the next, ending at 31. Row b of partners lists distinct blocks b - o with 1 <= o <= 7, -1 marking an unused slot; at most 4 slots are used, and in every draw some block uses all 4.
All inputs are finite; a program needn't handle non-finite values.
Results may differ from a plain program's by a relative error of at most 0.0049.
Values may be sent and summed in bfloat16 or wider, within the bound.
A program may use at most 128 MiB of HBM per device.

v0:
```python
import functools
import math

import jax
import jax.numpy as jnp
from jax import lax
from jax.experimental import pallas as pl
from jax.experimental.pallas import tpu as pltpu
from jax.sharding import PartitionSpec as P

MH = 128
P_SIZE = 64
NG = 8
N = 128
QH = 32
KVH = 4
HD = 128
WIN = 7
MAXP = 4
L = 128
HC = 8
NC = MH // HC
CW = HC * P_SIZE
UNITS = 16
UH = QH // UNITS
MESH = pl.DeviceIdType.MESH
F32 = jnp.float32
BF16 = jnp.bfloat16


def first_slot(b):
    return (b * 3) // 2


def expand(v):
    rows = v.shape[0]
    low = lax.broadcasted_iota(jnp.int32, (rows, 128), 1) < P_SIZE
    return jnp.concatenate(
        [
            jnp.where(
                low,
                jnp.broadcast_to(v[:, j : j + 1], (rows, 128)),
                jnp.broadcast_to(v[:, j + 1 : j + 2], (rows, 128)),
            )
            for j in range(0, HC, 2)
        ],
        axis=1,
    )


def kernel(
    nblk, x, z, bk, cq, dt, decay, skip, gain, q, k, v, rid_c, rid_r, partners,
    mix, att,
    state, yint, run_t, dt_t, rcol, scol, ecol, recv, send, kvbuf, own_bias,
    e_send, e_recv, kv_send, kv_recv,
):
    b = lax.axis_index("seq")
    grp = lax.axis_index("group")
    has_next = b + 1 < nblk
    has_prev = b > 0
    barrier = pltpu.get_barrier_semaphore()

    @pl.when(has_next)
    def _():
        pl.semaphore_signal(barrier, inc=1, device_id=(grp, b + 1), device_id_type=MESH)

    @pl.when(has_prev)
    def _():
        pl.semaphore_signal(barrier, inc=1, device_id=(grp, b - 1), device_id_type=MESH)

    row = lax.broadcasted_iota(jnp.int32, (L, L), 0)
    col = lax.broadcasted_iota(jnp.int32, (L, L), 1)
    causal = row >= col
    low = col < P_SIZE

    kvbuf[0, :, : KVH * HD] = k[...]
    kvbuf[0, :, KVH * HD :] = v[...]
    own_bias[...] = jnp.where(causal & (rid_c[...] == rid_r[...]), 0.0, -1e30)

    step = dt[...]
    running = jnp.dot(
        jnp.where(causal, 1.0, 0.0), -(decay[...] * step),
        precision=lax.Precision.HIGHEST, preferred_element_type=F32,
    )
    factor = step * jnp.exp(running[L - 1 : L, :] - running)
    grown = jnp.exp(running)
    run_t[...] = running.T
    dt_t[...] = step.T
    for c in range(NC):
        rcol[c] = running[:, c * HC : (c + 1) * HC]
        scol[c] = factor[:, c * HC : (c + 1) * HC]
        ecol[c] = grown[:, c * HC : (c + 1) * HC]

    @pl.when(jnp.logical_not(has_prev))
    def _():
        recv[...] = jnp.zeros_like(recv)

    ends = jnp.where(has_next, 0, 1) + jnp.where(has_prev, 0, 1)
    pl.semaphore_wait(barrier, 2 - ends)

    def wide(c):
        return pl.ds(pl.multiple_of(c * CW, CW), CW)

    def group_of(c):
        return pl.ds(pl.multiple_of((c // 2) * N, N), N)

    def kv_copy(r):
        return pltpu.make_async_remote_copy(
            src_ref=kvbuf.at[r - 1], dst_ref=kvbuf.at[r],
            send_sem=kv_send.at[r], recv_sem=kv_recv.at[r],
            device_id=(grp, b + 1), device_id_type=MESH,
        )

    def e_copy(c):
        return pltpu.make_async_remote_copy(
            src_ref=send.at[c], dst_ref=recv.at[c],
            send_sem=e_send.at[c], recv_sem=e_recv.at[c],
            device_id=(grp, b + 1), device_id_type=MESH,
        )

    def relay(r):
        @pl.when((r > 1) & (b >= r - 1))
        def _():
            kv_copy(jnp.maximum(r - 1, 1)).wait_recv()

        @pl.when((r <= WIN) & has_next & (b >= r - 1))
        def _():
            kv_copy(jnp.minimum(r, WIN)).start()

    def make_state(c, carry):
        xs = (x[:, wide(c)].astype(F32) * expand(scol[c])).astype(BF16)
        state[c] = lax.dot_general(
            bk[:, group_of(c)], xs, (((0,), (0,)), ((), ())), preferred_element_type=F32
        )
        return carry

    def forward(c):
        @pl.when(has_prev)
        def _():
            e_copy(c).wait_recv()

        @pl.when(has_next)
        def _():
            last = expand(ecol[c, L - 8 : L, :])[7:8, :]
            send[c] = (last * recv[c].astype(F32) + state[c]).astype(send.dtype)
            e_copy(c).start()

    def intra(c):
        cb = lax.dot_general(
            cq[:, group_of(c)], bk[:, group_of(c)], (((1,), (1,)), ((), ())),
            preferred_element_type=F32,
        )
        cb = jnp.where(causal, cb, 0.0)
        xc = x[:, wide(c)]
        cols = rcol[c]
        rows_r = run_t[pl.ds(pl.multiple_of(c * HC, HC), HC), :]
        rows_d = dt_t[pl.ds(pl.multiple_of(c * HC, HC), HC), :]

        def weight(j):
            gap = jnp.minimum(cols[:, j : j + 1] - rows_r[j : j + 1, :], 0.0)
            return (cb * jnp.exp(gap) * rows_d[j : j + 1, :]).astype(BF16)

        parts = []
        for j in range(0, HC, 2):
            xp = xc[:, j * P_SIZE : j * P_SIZE + 128]
            zero = jnp.zeros_like(xp)
            both = jnp.concatenate([jnp.where(low, xp, zero), jnp.where(low, zero, xp)], axis=0)
            w2 = jnp.concatenate([weight(j), weight(j + 1)], axis=1)
            parts.append(jnp.dot(w2, both, preferred_element_type=F32))
        yint[c] = jnp.concatenate(parts, axis=1) + skip[:, wide(c)] * xc.astype(F32)

    def attend(i):
        kh = (i * UH) // (QH // KVH)
        kcol = pl.ds(pl.multiple_of(kh * HD, HD), HD)
        vcol = pl.ds(pl.multiple_of((KVH + kh) * HD, HD), HD)
        keys = [kvbuf[0, :, kcol]]
        vals = [kvbuf[0, :, vcol]]
        bias = [own_bias[...]]
        for j in range(MAXP):
            p = partners[0, j]
            off = jnp.clip(jnp.where(p >= 0, b - p, 0), 0, WIN)
            keys.append(kvbuf[off, :, kcol])
            vals.append(kvbuf[off, :, vcol])
            bias.append(jnp.full((L, L), jnp.where(p >= 0, 0.0, -1e30), F32))
        keys = jnp.concatenate(keys, axis=0)
        vals = jnp.concatenate(vals, axis=0)
        bias = jnp.concatenate(bias, axis=1)
        for u in range(UH):
            hcol = pl.ds(pl.multiple_of((i * UH + u) * HD, HD), HD)
            s = lax.dot_general(
                q[:, hcol], keys, (((1,), (1,)), ((), ())), preferred_element_type=F32
            )
            s = s * (1.0 / math.sqrt(HD)) + bias
            e = jnp.exp(s - jnp.max(s, axis=1, keepdims=True))
            tot = jnp.sum(e, axis=1, keepdims=True)
            o = jnp.dot(e.astype(BF16), vals, preferred_element_type=F32)
            att[:, hcol] = (o / tot).astype(BF16)

    def finish(g, carry):
        ys = []
        total = None
        for half in range(2):
            c = 2 * g + half
            off = jnp.dot(
                cq[:, group_of(c)], recv[c].astype(BF16), preferred_element_type=F32
            )
            zc = z[:, wide(c)].astype(F32)
            y = (yint[c] + expand(ecol[c]) * off) * (zc / (1.0 + jnp.exp(-zc)))
            ys.append(y)
            part = jnp.sum(y * y, axis=1, keepdims=True)
            total = part if total is None else total + part
        inv = lax.rsqrt(total * (1.0 / (2 * CW)) + 1e-05)
        for half in range(2):
            c = 2 * g + half
            mix[:, wide(c)] = (ys[half] * inv * gain[:, wide(c)]).astype(BF16)
        return carry

    lax.fori_loop(0, NC, make_state, 0)
    begin = first_slot(b)

    def slot(s, carry):
        @pl.when((s % 2 == 0) & (s <= 2 * WIN))
        def _():
            relay(s // 2 + 1)

        c = s - begin

        @pl.when((c >= 0) & (c < NC))
        def _():
            forward(jnp.clip(c, 0, NC - 1))

        @pl.when(s < NC)
        def _():
            intra(jnp.minimum(s, NC - 1))

        @pl.when((s >= NC) & (s < NC + UNITS))
        def _():
            attend(jnp.clip(s - NC, 0, UNITS - 1))

        return carry

    lax.fori_loop(0, max(NC + UNITS, first_slot(nblk - 1) + NC), slot, 0)
    lax.fori_loop(0, NG, finish, 0)

    @pl.when(has_next)
    def _():
        def end_e(c, carry):
            e_copy(c).wait_send()
            return carry

        lax.fori_loop(0, NC, end_e, 0)

        def end_kv(r, carry):
            @pl.when(b >= r - 1)
            def _():
                kv_copy(r).wait_send()

            return carry

        lax.fori_loop(1, WIN + 1, end_kv, 0)


def shards(
    nblk, ssm_inputs, gate_inputs, write_keys, read_queries, step_size, decay_rate,
    skip_gain, norm_gain, query_proj, key_proj, value_proj, row_ids, partners,
):
    link = BF16 if nblk <= 32 else F32
    vmem = pl.BlockSpec(memory_space=pltpu.VMEM)
    return tuple(
        pl.pallas_call(
            functools.partial(kernel, nblk),
            out_shape=(
                jax.ShapeDtypeStruct((L, MH * P_SIZE), BF16),
                jax.ShapeDtypeStruct((L, QH * HD), BF16),
            ),
            in_specs=[vmem] * 13 + [pl.BlockSpec(memory_space=pltpu.SMEM)],
            out_specs=(vmem, vmem),
            scratch_shapes=[
                pltpu.VMEM((NC, N, CW), F32),
                pltpu.VMEM((NC, L, CW), F32),
                pltpu.VMEM((MH, L), F32),
                pltpu.VMEM((MH, L), F32),
                pltpu.VMEM((NC, L, HC), F32),
                pltpu.VMEM((NC, L, HC), F32),
                pltpu.VMEM((NC, L, HC), F32),
                pltpu.VMEM((NC, N, CW), link),
                pltpu.VMEM((NC, N, CW), link),
                pltpu.VMEM((WIN + 1, L, 2 * KVH * HD), BF16),
                pltpu.VMEM((L, L), F32),
                pltpu.SemaphoreType.DMA((NC,)),
                pltpu.SemaphoreType.DMA((NC,)),
                pltpu.SemaphoreType.DMA((WIN + 1,)),
                pltpu.SemaphoreType.DMA((WIN + 1,)),
            ],
            compiler_params=pltpu.CompilerParams(
                collective_id=0, has_side_effects=True, vmem_limit_bytes=52 * 1024 * 1024
            ),
            name="layer",
        )(
            ssm_inputs, gate_inputs, write_keys, read_queries, step_size,
            decay_rate[None, :], jnp.repeat(skip_gain, P_SIZE)[None, :], norm_gain[None, :],
            query_proj, key_proj, value_proj, row_ids[:, None], row_ids[None, :], partners,
        )
    )


def solution(mesh):
    rows = P(("group", "seq"), None)
    in_specs = (
        rows, rows, rows, rows, rows, P(), P(), P(), rows, rows, rows, P(("group", "seq")), rows,
    )
    return jax.shard_map(
        functools.partial(shards, mesh.shape["seq"]),
        mesh=mesh, in_specs=in_specs, out_specs=(rows, rows), check_vma=False,
    )
```

profile of v0, /device:TPU:31, one launch (start us, length us, event | category | flops | bytes accessed | tf_op | source)
XLA Modules:
  0.0 96.7 jit_solution(10511337021994291178)
XLA Ops:
  0.6 0.7 broadcast_in_dim.16
  1.4 0.1 broadcast_in_dim_reshape.3.skip
  1.5 0.8 copy.16.rid_c
  2.2 0.0 copy-start
  2.2 0.9 copy-done
  3.2 0.0 copy-start.1
  3.2 0.9 copy-done.1
  4.1 0.0 copy-start.2
  4.1 0.9 copy-done.2
  5.0 0.0 copy-start.3
  5.0 0.9 copy-done.3
  5.9 0.0 copy-start.4
  5.9 0.8 copy-done.4
  6.8 0.0 copy-start.5
  6.8 0.8 copy-done.5
  7.5 0.0 copy-start.6
  7.5 0.7 copy-done.6
  8.2 0.7 copy-done.7
  8.9 0.7 copy-done.8
  9.5 83.0 %layer.1 = (bf16[128,8192]{1,0:T(8,128)(2,1)}, bf16[128,4096]{1,0:T(8,128)(2,1)}) custom-call(bf16[128,8192]{1,0:T(8,128)(2,1)} %x.1, bf16[128,8192]{1,0:T(8,128)(2,1)} %z.1, bf16[128,1024]{1,0:T(8,128)(2,1)S(1)} %copy-done, bf16[128,1024]{1,0:T(8,128)(2,1)S(1)} %copy-done.1, f32[128,128]{1,0:T(8,128)S(1)} %copy-done.4, f32[1,128]{1,0:T(1,128)S(1)} %bitcast.7, ...), custom_call_target="tpu_custom_call" | custom-call | tf_op jit(solution)/shard_map/layer/pallas_call | solution.py:270
  92.5 0.0 copy-start.9
  92.5 3.2 %copy.19 = bf16[128,8192]{1,0:T(8,128)(2,1)} copy(bf16[128,8192]{1,0:T(8,128)(2,1)} %get-tuple-element.4) | data formatting | bytes 4194304
  95.7 0.0 copy-done.9
  95.7 1.0 %copy.20 = bf16[128,4096]{1,0:T(8,128)(2,1)} copy(bf16[128,4096]{1,0:T(8,128)(2,1)S(1)} %copy-done.9) | data formatting | bytes 2097152
  (2 shorter events, 0.0 us)
Async XLA Ops:
  2.2 0.9 copy-start
  3.2 0.9 copy-start.1
  4.1 0.9 copy-start.2
  5.0 0.9 copy-start.3
  5.9 0.8 copy-start.4
  6.8 0.8 copy-start.5
  7.5 0.7 copy-start.6
  8.2 0.7 copy-start.7
  8.9 0.7 copy-start.8
  92.5 3.2 %copy-start.9 = (bf16[128,4096]{1,0:T(8,128)(2,1)S(1)}, bf16[128,4096]{1,0:T(8,128)(2,1)}, u32[]{:S(2)}) copy-start(bf16[128,4096]{1,0:T(8,128)(2,1)} %get-tuple-element.5) | copy-start | bytes 3145732
where the time goes:
time: 97.1 us; the launch traced here: 96.7 us
  Pallas kernels  83 us (85%)
  local copies, waits for them, and re-layouts  13 us (13%)
    pallas_call x1, Pallas kernels, shards(): pl.pallas_call(functools.partial(kernel, nblk), out_shape=(jax.ShapeDtype...  83 us
    unnamed x22, local copies, waits for them, and re-layouts  11.4 us

commit v1 on v0

--- a/solution.py
+++ b/solution.py
@@ -22,6 +22,7 @@
 NC = MH // HC
 CW = HC * P_SIZE
 UNITS = 16
+LATEST = NC + UNITS - NC // 2
 UH = QH // UNITS
 MESH = pl.DeviceIdType.MESH
 F32 = jnp.float32
@@ -29,7 +30,7 @@
 
 
 def first_slot(b):
-    return (b * 3) // 2
+    return jnp.minimum((b * 8) // 5, LATEST)
 
 
 def expand(v):
@@ -196,7 +197,7 @@
             o = jnp.dot(e.astype(BF16), vals, preferred_element_type=F32)
             att[:, hcol] = (o / tot).astype(BF16)
 
-    def finish(g, carry):
+    def finish(g):
         ys = []
         total = None
         for half in range(2):
@@ -213,7 +214,6 @@
         for half in range(2):
             c = 2 * g + half
             mix[:, wide(c)] = (ys[half] * inv * gain[:, wide(c)]).astype(BF16)
-        return carry
 
     lax.fori_loop(0, NC, make_state, 0)
     begin = first_slot(b)
@@ -229,18 +229,27 @@
         def _():
             forward(jnp.clip(c, 0, NC - 1))
 
-        @pl.when(s < NC)
-        def _():
-            intra(jnp.minimum(s, NC - 1))
-
-        @pl.when((s >= NC) & (s < NC + UNITS))
-        def _():
-            attend(jnp.clip(s - NC, 0, UNITS - 1))
+        passing = (c >= 0) & (c < NC)
+        unit = jnp.where(c < 0, s, jnp.where(passing, begin + c // 2, s - NC // 2))
+        works = jnp.logical_not(passing) | (c % 2 == 0)
+
+        @pl.when(works & (unit < NC))
+        def _():
+            intra(jnp.minimum(unit, NC - 1))
+
+        @pl.when(works & (unit >= NC) & (unit < NC + UNITS))
+        def _():
+            attend(jnp.clip(unit - NC, 0, UNITS - 1))
+
+        done = s - LATEST - 1
+
+        @pl.when((done >= 0) & (done % 2 == 0))
+        def _():
+            finish(jnp.clip(done // 2, 0, NG - 1))
 
         return carry
 
-    lax.fori_loop(0, max(NC + UNITS, first_slot(nblk - 1) + NC), slot, 0)
-    lax.fori_loop(0, NG, finish, 0)
+    lax.fori_loop(0, LATEST + NC, slot, 0)
 
     @pl.when(has_next)
     def _():

time: 97.1 us -> 92.6 us (0.954)
  Pallas kernels: 83 us -> 77.6 us
    pallas_call x1, Pallas kernels: 83 us -> 77.6 us  [shards(): pl.pallas_call(functools.partial(kernel, nblk), out_shape=(jax.ShapeDtype...]
where the time goes in v1:
time: 92.6 us; the launch traced here: 91.3 us
  Pallas kernels  77.6 us (84%)
  local copies, waits for them, and re-layouts  13 us (14%)
    pallas_call x1, Pallas kernels, shards(): pl.pallas_call(functools.partial(kernel, nblk), out_shape=(jax.ShapeDtype...  77.6 us
    unnamed x22, local copies, waits for them, and re-layouts  11.4 us

profile of v1, /device:TPU:31, one launch (start us, length us, event | category | flops | bytes accessed | tf_op | source)
XLA Modules:
  0.0 91.3 jit_solution(1885011283269206846)
XLA Ops:
  0.6 0.7 broadcast_in_dim.16
  1.4 0.1 broadcast_in_dim_reshape.3.skip
  1.5 0.8 copy.16.rid_c
  2.2 0.0 copy-start
  2.2 0.9 %copy-done = bf16[128,1024]{1,0:T(8,128)(2,1)S(1)} copy-done((bf16[128,1024]{1,0:T(8,128)(2,1)S(1)}, bf16[128,1024]{1,0:T(8,128)(2,1)}, u32[]{:S(2)}) %copy-start) | copy-done | bytes 262168
  3.2 0.0 copy-start.1
  3.2 0.9 %copy-done.1 = bf16[128,1024]{1,0:T(8,128)(2,1)S(1)} copy-done((bf16[128,1024]{1,0:T(8,128)(2,1)S(1)}, bf16[128,1024]{1,0:T(8,128)(2,1)}, u32[]{:S(2)}) %copy-start.1) | copy-done | bytes 262168
  4.1 0.0 copy-start.2
  4.1 0.9 copy-done.2
  5.0 0.0 copy-start.3
  5.0 0.9 copy-done.3
  5.9 0.0 copy-start.4
  5.9 0.8 copy-done.4
  6.8 0.0 copy-start.5
  6.8 0.8 copy-done.5
  7.5 0.0 copy-start.6
  7.5 0.7 copy-done.6
  8.2 0.7 copy-done.7
  8.9 0.7 copy-done.8
  9.5 77.6 %layer.1 = (bf16[128,8192]{1,0:T(8,128)(2,1)}, bf16[128,4096]{1,0:T(8,128)(2,1)}) custom-call(bf16[128,8192]{1,0:T(8,128)(2,1)} %x.1, bf16[128,8192]{1,0:T(8,128)(2,1)} %z.1, bf16[128,1024]{1,0:T(8,128)(2,1)S(1)} %copy-done, bf16[128,1024]{1,0:T(8,128)(2,1)S(1)} %copy-done.1, f32[128,128]{1,0:T(8,128)S(1)} %copy-done.4, f32[1,128]{1,0:T(1,128)S(1)} %bitcast.7, ...), custom_call_target="tpu_custom_call" | custom-call | tf_op jit(solution)/shard_map/layer/pallas_call | solution.py:279
  87.1 0.0 copy-start.9
  87.2 3.2 %copy.19 = bf16[128,8192]{1,0:T(8,128)(2,1)} copy(bf16[128,8192]{1,0:T(8,128)(2,1)} %get-tuple-element.4) | data formatting | bytes 4194304
  90.3 0.0 copy-done.9
  90.3 1.0 %copy.20 = bf16[128,4096]{1,0:T(8,128)(2,1)} copy(bf16[128,4096]{1,0:T(8,128)(2,1)S(1)} %copy-done.9) | data formatting | bytes 2097152
  (2 shorter events, 0.0 us)
Async XLA Ops:
  2.2 0.9 %copy-start = (bf16[128,1024]{1,0:T(8,128)(2,1)S(1)}, bf16[128,1024]{1,0:T(8,128)(2,1)}, u32[]{:S(2)}) copy-start(bf16[128,1024]{1,0:T(8,128)(2,1)} %bk.1) | copy-start | bytes 786436
  3.2 0.9 %copy-start.1 = (bf16[128,1024]{1,0:T(8,128)(2,1)S(1)}, bf16[128,1024]{1,0:T(8,128)(2,1)}, u32[]{:S(2)}) copy-start(bf16[128,1024]{1,0:T(8,128)(2,1)} %cq.1) | copy-start | bytes 786436
  4.1 0.9 copy-start.2
  5.0 0.9 copy-start.3
  5.9 0.8 copy-start.4
  6.8 0.8 copy-start.5
  7.5 0.7 copy-start.6
  8.2 0.7 copy-start.7
  8.9 0.7 copy-start.8
  87.1 3.2 %copy-start.9 = (bf16[128,4096]{1,0:T(8,128)(2,1)S(1)}, bf16[128,4096]{1,0:T(8,128)(2,1)}, u32[]{:S(2)}) copy-start(bf16[128,4096]{1,0:T(8,128)(2,1)} %get-tuple-element.5) | copy-start | bytes 3145732

commit v2 on v1

--- a/solution.py
+++ b/solution.py
@@ -22,7 +22,7 @@
 NC = MH // HC
 CW = HC * P_SIZE
 UNITS = 16
-LATEST = NC + UNITS - NC // 2
+LATEST = NC + UNITS
 UH = QH // UNITS
 MESH = pl.DeviceIdType.MESH
 F32 = jnp.float32
@@ -30,7 +30,7 @@
 
 
 def first_slot(b):
-    return jnp.minimum((b * 8) // 5, LATEST)
+    return jnp.minimum(2 * b, LATEST)
 
 
 def expand(v):

time: 92.6 us -> 90.7 us (0.979)
  Pallas kernels: 77.6 us -> 76.6 us
    pallas_call x1, Pallas kernels: 77.6 us -> 76.6 us  [shards(): pl.pallas_call(functools.partial(kernel, nblk), out_shape=(jax.ShapeDtype...]
where the time goes in v2:
time: 90.7 us; the launch traced here: 90.3 us
  Pallas kernels  76.6 us (84%)
  local copies, waits for them, and re-layouts  13 us (14%)
    pallas_call x1, Pallas kernels, shards(): pl.pallas_call(functools.partial(kernel, nblk), out_shape=(jax.ShapeDtype...  76.6 us
    unnamed x22, local copies, waits for them, and re-layouts  11.4 us

profile of v2, /device:TPU:31, one launch (start us, length us, event | category | flops | bytes accessed | tf_op | source)
XLA Modules:
  0.0 90.3 jit_solution(3550170185794799478)
XLA Ops:
  0.6 0.7 broadcast_in_dim.16
  1.4 0.1 broadcast_in_dim_reshape.3.skip
  1.5 0.8 copy.16.rid_c
  2.2 0.0 copy-start
  2.2 0.9 %copy-done = bf16[128,1024]{1,0:T(8,128)(2,1)S(1)} copy-done((bf16[128,1024]{1,0:T(8,128)(2,1)S(1)}, bf16[128,1024]{1,0:T(8,128)(2,1)}, u32[]{:S(2)}) %copy-start) | copy-done | bytes 262168
  3.2 0.0 copy-start.1
  3.2 0.9 %copy-done.1 = bf16[128,1024]{1,0:T(8,128)(2,1)S(1)} copy-done((bf16[128,1024]{1,0:T(8,128)(2,1)S(1)}, bf16[128,1024]{1,0:T(8,128)(2,1)}, u32[]{:S(2)}) %copy-start.1) | copy-done | bytes 262168
  4.1 0.0 copy-start.2
  4.1 0.9 copy-done.2
  5.0 0.0 copy-start.3
  5.0 0.9 copy-done.3
  5.9 0.0 copy-start.4
  5.9 0.8 copy-done.4
  6.8 0.0 copy-start.5
  6.8 0.8 copy-done.5
  7.5 0.0 copy-start.6
  7.5 0.7 copy-done.6
  8.2 0.7 copy-done.7
  8.9 0.7 copy-done.8
  9.5 76.6 %layer.1 = (bf16[128,8192]{1,0:T(8,128)(2,1)}, bf16[128,4096]{1,0:T(8,128)(2,1)}) custom-call(bf16[128,8192]{1,0:T(8,128)(2,1)} %x.1, bf16[128,8192]{1,0:T(8,128)(2,1)} %z.1, bf16[128,1024]{1,0:T(8,128)(2,1)S(1)} %copy-done, bf16[128,1024]{1,0:T(8,128)(2,1)S(1)} %copy-done.1, f32[128,128]{1,0:T(8,128)S(1)} %copy-done.4, f32[1,128]{1,0:T(1,128)S(1)} %bitcast.7, ...), custom_call_target="tpu_custom_call" | custom-call | tf_op jit(solution)/shard_map/layer/pallas_call | solution.py:279
  86.1 0.0 copy-start.9
  86.2 3.2 %copy.19 = bf16[128,8192]{1,0:T(8,128)(2,1)} copy(bf16[128,8192]{1,0:T(8,128)(2,1)} %get-tuple-element.4) | data formatting | bytes 4194304
  89.3 0.0 copy-done.9
  89.3 1.0 %copy.20 = bf16[128,4096]{1,0:T(8,128)(2,1)} copy(bf16[128,4096]{1,0:T(8,128)(2,1)S(1)} %copy-done.9) | data formatting | bytes 2097152
  (2 shorter events, 0.0 us)
Async XLA Ops:
  2.2 0.9 %copy-start = (bf16[128,1024]{1,0:T(8,128)(2,1)S(1)}, bf16[128,1024]{1,0:T(8,128)(2,1)}, u32[]{:S(2)}) copy-start(bf16[128,1024]{1,0:T(8,128)(2,1)} %bk.1) | copy-start | bytes 786436
  3.2 0.9 %copy-start.1 = (bf16[128,1024]{1,0:T(8,128)(2,1)S(1)}, bf16[128,1024]{1,0:T(8,128)(2,1)}, u32[]{:S(2)}) copy-start(bf16[128,1024]{1,0:T(8,128)(2,1)} %cq.1) | copy-start | bytes 786436
  4.1 0.9 %copy-start.2 = (bf16[128,512]{1,0:T(8,128)(2,1)S(1)}, bf16[128,512]{1,0:T(8,128)(2,1)}, u32[]{:S(2)}) copy-start(bf16[128,512]{1,0:T(8,128)(2,1)} %k.1) | copy-start | bytes 393220
  5.0 0.9 %copy-start.3 = (bf16[128,512]{1,0:T(8,128)(2,1)S(1)}, bf16[128,512]{1,0:T(8,128)(2,1)}, u32[]{:S(2)}) copy-start(bf16[128,512]{1,0:T(8,128)(2,1)} %v.1) | copy-start | bytes 393220
  5.9 0.8 copy-start.4
  6.8 0.8 copy-start.5
  7.5 0.7 copy-start.6
  8.2 0.7 copy-start.7
  8.9 0.7 copy-start.8
  86.1 3.2 %copy-start.9 = (bf16[128,4096]{1,0:T(8,128)(2,1)S(1)}, bf16[128,4096]{1,0:T(8,128)(2,1)}, u32[]{:S(2)}) copy-start(bf16[128,4096]{1,0:T(8,128)(2,1)} %get-tuple-element.5) | copy-start | bytes 3145732

commit v3 on v2

--- a/solution.py
+++ b/solution.py
@@ -302,7 +302,7 @@
                 pltpu.SemaphoreType.DMA((WIN + 1,)),
             ],
             compiler_params=pltpu.CompilerParams(
-                collective_id=0, has_side_effects=True, vmem_limit_bytes=52 * 1024 * 1024
+                collective_id=0, has_side_effects=True, vmem_limit_bytes=63 * 1024 * 1024
             ),
             name="layer",
         )(

time: 90.7 us -> 84.7 us (0.934)
  local copies, waits for them, and re-layouts: 13 us -> 7 us
    unnamed x22 -> x4, local copies, waits for them, and re-layouts: 11.4 us -> 4.16 us
where the time goes in v3:
time: 84.7 us; the launch traced here: 84.6 us
  Pallas kernels  76.9 us (91%)
  local copies, waits for them, and re-layouts  7 us (8%)
    pallas_call x1, Pallas kernels, shards(): pl.pallas_call(functools.partial(kernel, nblk), out_shape=(jax.ShapeDtype...  76.9 us
    unnamed x4, local copies, waits for them, and re-layouts  4.16 us

profile of v3, /device:TPU:31, one launch (start us, length us, event | category | flops | bytes accessed | tf_op | source)
XLA Modules:
  0.0 84.6 jit_solution(14784617295036596175)
XLA Ops:
  0.6 0.7 broadcast_in_dim.16
  1.4 0.7 broadcast_in_dim_reshape.3.skip
  2.1 1.4 %copy.16.rid_c = s32[128,1]{1,0:T(8,128)} copy(s32[128,1]{0,1:T(1,128)} %bitcast.5) | data formatting | bytes 1024 | tf_op jit(solution)/shard_map/broadcast_in_dim | solution.py:311
  3.5 76.9 %layer.1 = (bf16[128,8192]{1,0:T(8,128)(2,1)}, bf16[128,4096]{1,0:T(8,128)(2,1)}) custom-call(bf16[128,8192]{1,0:T(8,128)(2,1)} %x.1, bf16[128,8192]{1,0:T(8,128)(2,1)} %z.1, bf16[128,1024]{1,0:T(8,128)(2,1)} %bk.1, bf16[128,1024]{1,0:T(8,128)(2,1)} %cq.1, f32[128,128]{1,0:T(8,128)} %dt.1, f32[1,128]{1,0:T(1,128)} %bitcast.7, ...), custom_call_target="tpu_custom_call" | custom-call | tf_op jit(solution)/shard_map/layer/pallas_call | solution.py:279
  80.4 0.0 copy-start
  80.4 3.2 %copy.19 = bf16[128,8192]{1,0:T(8,128)(2,1)} copy(bf16[128,8192]{1,0:T(8,128)(2,1)} %get-tuple-element.4) | data formatting | bytes 4194304
  83.6 0.0 copy-done
  83.6 1.0 %copy.20 = bf16[128,4096]{1,0:T(8,128)(2,1)} copy(bf16[128,4096]{1,0:T(8,128)(2,1)S(1)} %copy-done) | data formatting | bytes 2097152
Async XLA Ops:
  80.4 3.2 %copy-start = (bf16[128,4096]{1,0:T(8,128)(2,1)S(1)}, bf16[128,4096]{1,0:T(8,128)(2,1)}, u32[]{:S(2)}) copy-start(bf16[128,4096]{1,0:T(8,128)(2,1)} %get-tuple-element.5) | copy-start | bytes 3145732
